TPU v7x, 32 devices: a whole 2x2x4 slice. The times are simulated.
32 devices in a mesh: lat: 4 (over x, core), lon: 8 (over z, y).
Axes of the slice: x: 2, y: 2, z: 4, core: 2. Of those that a mesh axis runs over, the one named last changes fastest.
Arguments:
- grid_latent: bfloat16 [16, 1024, 512], P('lat', 'lon'), may hold values from -6 to 6
- mesh_latent: bfloat16 [4096, 512], P(('lat', 'lon')), may hold values from -6 to 6
- g2m_edges: bfloat16 [65536, 512], P(('lat', 'lon')), may hold values from -6 to 6
- g2m_senders: int32 [32, 2048], P(('lat', 'lon')), may hold values from 0 to 1631, as said below
- g2m_receivers: int32 [32, 2048], P(('lat', 'lon')), may hold values from 0 to 127, as said below
- mm_edges: bfloat16 [65536, 512], P(('lat', 'lon')), may hold values from -6 to 6
- mm_senders: int32 [32, 2048], P(('lat', 'lon')), may hold values from 0 to 639
- mm_receivers: int32 [32, 2048], P(('lat', 'lon')), may hold values from 0 to 128, as said below
- send_rows: int32 [32, 512], P(('lat', 'lon')), may hold values from 0 to 127
- edge_in: bfloat16 [3, 3, 512, 512], replicated, may hold values from -0.15625 to 0.15625
- edge_out: bfloat16 [3, 512, 512], replicated, may hold values from -0.25 to 0.25
- node_in: bfloat16 [3, 2, 512, 512], replicated, may hold values from -0.1875 to 0.1875
- node_out: bfloat16 [3, 512, 512], replicated, may hold values from -0.25 to 0.25
- norm_gain: float32 [3, 2, 512], replicated, may hold values from 0.5 to 1.5
- norm_bias: float32 [3, 2, 512], replicated, may hold values from -1.5 to 1.5
Outputs:
- mesh_out: bfloat16 [4096, 512], P(('lat', 'lon'))
Inputs may be any that keep to these rules, and one draw needn't show every extreme that they name: `g2m_receivers`: each patch's edges are sorted by receiver; every mesh node of a patch receives at least one grid-to-mesh edge; the sender cell lies within 4 rows and columns of a cell that is fixed for the receiving node. `g2m_senders`: A flat index into the tile extended by 4 cells, with rows of 136 cells. `mm_receivers`: sorted within a patch; the used slots come first and the unused ones hold 128; some patch uses all 2048 slots in every draw.
All inputs are finite; a program needn't handle non-finite values.
Results may differ from a plain program's by a relative error of at most 0.012.
Values may be sent and summed in bfloat16 or wider, within the bound.
A program may use at most 128 MiB of HBM per device.

v0:
```python
import math

import jax
import jax.numpy as jnp
from jax import lax
from jax.sharding import PartitionSpec as P

HALO = 4


NORM_EPS = 1e-05


def padded_2(array, sides, width, wrap):
    for axis, dim in sides:
        size, length = (lax.axis_size(axis), array.shape[dim])
        up = [(i, (i + 1) % size) for i in range(size if wrap else size - 1)]
        down = [(j, i) for i, j in up]
        last = lax.slice_in_dim(array, length - width, length, axis=dim)
        leading = lax.slice_in_dim(array, 0, width, axis=dim)
        before = lax.ppermute(last, axis, up)
        after = lax.ppermute(leading, axis, down)
        array = jnp.concatenate([before, array, after], axis=dim)
    return array


def normalize(values, gains, biases):
    centre = jnp.mean(values, axis=-1, keepdims=True)
    spread = jnp.mean(jnp.square(values - centre), axis=-1, keepdims=True)
    return (values - centre) * lax.rsqrt(spread + NORM_EPS) * gains + biases


def project(values, weights):
    return jnp.dot(values, weights, preferred_element_type=jnp.float32).astype(jnp.bfloat16)


def edge_update(edge_rows, sender_terms, receiver_terms, weights_in, weights_out, gains, biases):
    pre_act = jnp.dot(edge_rows, weights_in, preferred_element_type=jnp.float32)
    pre_act = pre_act + sender_terms.astype(jnp.float32) + receiver_terms.astype(jnp.float32)
    hidden = jax.nn.silu(pre_act).astype(jnp.bfloat16)
    output = jnp.dot(hidden, weights_out, preferred_element_type=jnp.float32)
    return (edge_rows.astype(jnp.float32) + normalize(output, gains, biases)).astype(jnp.bfloat16)


def node_update(nodes, summed, weights_in, weights_out, gains, biases):
    pre_act = jnp.dot(nodes, weights_in[0], preferred_element_type=jnp.float32)
    pre_act = pre_act + jnp.dot(
        summed.astype(jnp.bfloat16), weights_in[1], preferred_element_type=jnp.float32
    )
    hidden = jax.nn.silu(pre_act).astype(jnp.bfloat16)
    output = jnp.dot(hidden, weights_out, preferred_element_type=jnp.float32)
    return (nodes.astype(jnp.float32) + normalize(output, gains, biases)).astype(jnp.bfloat16)


def pick_rows(table, indices):
    count = indices.shape[0]
    block_rows = math.gcd(count, 512)
    table_rows = jnp.arange(table.shape[0], dtype=jnp.int32)

    def one_block(piece):
        selector = (piece[:, None] == table_rows[None, :]).astype(table.dtype)
        return jnp.dot(selector, table, preferred_element_type=jnp.float32).astype(table.dtype)

    picked = lax.map(one_block, indices.reshape(-1, block_rows))
    return picked.reshape(count, table.shape[1])


def incidence_sum(edge_rows, receivers, node_count):
    incidence = (jnp.arange(node_count, dtype=jnp.int32)[:, None] == receivers[None, :]).astype(
        jnp.bfloat16
    )
    return jnp.dot(incidence, edge_rows, preferred_element_type=jnp.float32)


def local(
    grid_latent,
    mesh_latent,
    g2m_edges,
    g2m_senders,
    g2m_receivers,
    mm_edges,
    mm_senders,
    mm_receivers,
    send_rows,
    edge_in,
    edge_out,
    node_in,
    node_out,
    norm_gain,
    norm_bias,
):
    features = grid_latent.shape[-1]
    node_count = mesh_latent.shape[0]
    widened = padded_2(grid_latent, (("lon", 1),), HALO, True)
    padded = padded_2(widened, (("lat", 0),), HALO, False)
    flat_tile = padded.reshape(-1, features)
    lookup = project(flat_tile, edge_in[0, 1])
    sent = pick_rows(lookup, g2m_senders[0])
    receiver_table = project(mesh_latent, edge_in[0, 2])
    got = pick_rows(receiver_table, g2m_receivers[0])
    encoded = edge_update(
        g2m_edges, sent, got, edge_in[0, 0], edge_out[0], norm_gain[0, 0], norm_bias[0, 0]
    )
    summed = incidence_sum(encoded, g2m_receivers[0], node_count)
    mesh_nodes = node_update(
        mesh_latent, summed, node_in[0], node_out[0], norm_gain[0, 1], norm_bias[0, 1]
    )
    receivers = mm_receivers[0]
    clipped = jnp.minimum(receivers, node_count - 1)
    edge_state = mm_edges
    for level in range(1, edge_in.shape[0]):
        outgoing = project(mesh_nodes, edge_in[level, 1])
        out_rows = pick_rows(outgoing, send_rows[0])
        arrived = lax.all_to_all(out_rows, ("lat", "lon"), split_axis=0, concat_axis=0, tiled=True)
        combined = jnp.concatenate([outgoing, arrived], axis=0)
        sent = pick_rows(combined, mm_senders[0])
        recv_table = project(mesh_nodes, edge_in[level, 2])
        got = pick_rows(recv_table, clipped)
        edge_state = edge_update(
            edge_state,
            sent,
            got,
            edge_in[level, 0],
            edge_out[level],
            norm_gain[level, 0],
            norm_bias[level, 0],
        )
        summed = incidence_sum(edge_state, receivers, node_count)
        mesh_nodes = node_update(
            mesh_nodes,
            summed,
            node_in[level],
            node_out[level],
            norm_gain[level, 1],
            norm_bias[level, 1],
        )
    return mesh_nodes


def solution(mesh):
    in_specs = (
        P("lat", "lon", None),
        P(("lat", "lon"), None),
        P(("lat", "lon"), None),
        P(("lat", "lon"), None),
        P(("lat", "lon"), None),
        P(("lat", "lon"), None),
        P(("lat", "lon"), None),
        P(("lat", "lon"), None),
        P(("lat", "lon"), None),
        P(),
        P(),
        P(),
        P(),
        P(),
        P(),
    )
    out_specs = P(("lat", "lon"), None)
    return jax.shard_map(local, mesh=mesh, in_specs=in_specs, out_specs=out_specs, check_vma=False)
```

profile of v0, /device:TPU:0, one launch (start us, length us, event | category | flops | bytes accessed | tf_op | source)
XLA Modules:
  0.0 165.2 jit_solution(17750369767327097111)
XLA Ops:
  0.8 3.0 %collective-permute-start = (bf16[4,4,512]{2,1,0:T(4,128)(2,1)S(1)}, bf16[4,4,512]{2,1,0:T(4,128)(2,1)S(1)}, u32[]{:S(2)}, u32[]{:S(2)}) collective-permute-start(bf16[4,4,512]{2,1,0:T(4,128)(2,1)S(1)} %get-tuple-element.311), channel_id=1, source_target_pairs={{0,1},{1,2},{2,3},{3,4},{4,5},{5,6},{6,7},{7,0},{8,9},{9,10},{10,1... | collective-permute-start | bytes 49160 | tf_op jit(solution)/shard_map/ppermute | solution.py:21
  3.8 3.1 %collective-permute-start.1 = (bf16[4,4,512]{2,1,0:T(4,128)(2,1)S(1)}, bf16[4,4,512]{2,1,0:T(4,128)(2,1)S(1)}, u32[]{:S(2)}, u32[]{:S(2)}) collective-permute-start(bf16[4,4,512]{2,1,0:T(4,128)(2,1)S(1)} %get-tuple-element.312), channel_id=1, source_target_pairs={{1,0},{2,1},{3,2},{4,3},{5,4},{6,5},{7,6},{0,7},{9,8},{10,9},{11,1... | collective-permute-start | bytes 49160 | tf_op jit(solution)/shard_map/ppermute | solution.py:22
  10.5 1.5 while.75
  13.4 4.1 %copy.16 = bf16[2048,512]{0,1:T(8,128)(2,1)} copy(bf16[2048,512]{1,0:T(8,128)(2,1)} %param.29) | data formatting | bytes 4194304 | tf_op args[2]
  22.1 3.0 %copy.17 = bf16[2048,512]{0,1:T(8,128)(2,1)S(1)} copy(bf16[2048,512]{1,0:T(8,128)(2,1)} %param.32) | data formatting | bytes 4194304 | tf_op args[5]
  25.7 2.0 %fusion.71 = f32[128,512]{1,0:T(8,128)} fusion(bf16[128,512]{1,0:T(8,128)(2,1)S(1)} %copy-done.7, bf16[3,2,512,512]{3,2,1,0:T(8,128)(2,1)} %param.38), kind=kOutput, calls=%fused_computation.110 | convolution fusion | flops 67108864 | bytes 917504 | tf_op jit(solution)/shard_map/dot_general | solution.py:46
  28.9 3.3 %convolution_convert_fusion.3 = bf16[1632,512]{1,0:T(8,128)(2,1)} fusion(bf16[1632,512]{1,0:T(8,128)(2,1)S(1)} %bitcast.220, bf16[3,3,512,512]{3,2,1,0:T(8,128)(2,1)} %param.36), kind=kOutput, calls=%fused_computation.60 | convolution fusion | flops 856473600 | bytes 3866624 | tf_op jit(solution)/shard_map/dot_general | solution.py:34
  32.2 1.6 broadcast.135.clone.1
  33.7 13.7 %while.74 = (s32[]{:T(128)}, bf16[4,512,512]{2,1,0:T(8,128)(2,1)}, s32[4,512]{1,0:T(4,128)S(1)}, bf16[1632,512]{1,0:T(8,128)(2,1)}, s32[]{:T(128)}) while((s32[]{:T(128)}, bf16[4,512,512]{2,1,0:T(8,128)(2,1)}, s32[4,512]{1,0:T(4,128)S(1)}, bf16[1632,512]{1,0:T(8,128)(2,1)}, s32[]{:T(128)}) %tuple.125), condition=%wide.region_1.2_spmd.clone, body=%wide.region_0.1_spmd.clone.sunk | while | flops 856735744 | bytes 2202177 | solution.py:64
  33.7 3.4 %fusion.166 = bf16[4,512,512]{2,1,0:T(8,128)(2,1)} fusion(bf16[4,512,512]{2,1,0:T(8,128)(2,1)} %get-tuple-element.508, s32[]{:T(128)} %get-tuple-element.507, bf16[1632,512]{1,0:T(8,128)(2,1)} %get-tuple-element.515, s32[512]{0:T(512)S(1)} %bitcast.224), kind=kOutput, calls=%fused_computation.11.clone.1 | convolution fusion | flops 856735744 | bytes 2198016 | tf_op jit(solution)/shard_map/while/body/eval_jaxpr/dot_general | solution.py:62
  37.2 3.5 %fusion.166 = bf16[4,512,512]{2,1,0:T(8,128)(2,1)} fusion(bf16[4,512,512]{2,1,0:T(8,128)(2,1)} %get-tuple-element.508, s32[]{:T(128)} %get-tuple-element.507, bf16[1632,512]{1,0:T(8,128)(2,1)} %get-tuple-element.515, s32[512]{0:T(512)S(1)} %bitcast.224), kind=kOutput, calls=%fused_computation.11.clone.1 | convolution fusion | flops 856735744 | bytes 2198016 | tf_op jit(solution)/shard_map/while/body/eval_jaxpr/dot_general | solution.py:62
  40.7 3.4 %fusion.166 = bf16[4,512,512]{2,1,0:T(8,128)(2,1)} fusion(bf16[4,512,512]{2,1,0:T(8,128)(2,1)} %get-tuple-element.508, s32[]{:T(128)} %get-tuple-element.507, bf16[1632,512]{1,0:T(8,128)(2,1)} %get-tuple-element.515, s32[512]{0:T(512)S(1)} %bitcast.224), kind=kOutput, calls=%fused_computation.11.clone.1 | convolution fusion | flops 856735744 | bytes 2198016 | tf_op jit(solution)/shard_map/while/body/eval_jaxpr/dot_general | solution.py:62
  44.1 3.4 %fusion.166 = bf16[4,512,512]{2,1,0:T(8,128)(2,1)} fusion(bf16[4,512,512]{2,1,0:T(8,128)(2,1)} %get-tuple-element.508, s32[]{:T(128)} %get-tuple-element.507, bf16[1632,512]{1,0:T(8,128)(2,1)} %get-tuple-element.515, s32[512]{0:T(512)S(1)} %bitcast.224), kind=kOutput, calls=%fused_computation.11.clone.1 | convolution fusion | flops 856735744 | bytes 2198016 | tf_op jit(solution)/shard_map/while/body/eval_jaxpr/dot_general | solution.py:62
  47.5 8.0 %fusion.117 = (f32[2048]{0:T(1024)S(1)}, f32[2048,512]{0,1:T(8,128)}) fusion(bf16[3,512,512]{2,1,0:T(8,128)(2,1)} %param.37, bf16[2048,512]{1,0:T(8,128)(2,1)} %bitcast.213, bf16[2048,512]{1,0:T(8,128)(2,1)} %bitcast.214, bf16[2048,512]{1,0:T(8,128)(2,1)} %param.29, bf16[3,3,512,512]{3,2,1,0:T(8,128)(2,1)} %param.36), kind=kOutput, calls=%fused_computation.167 | convolution fusion | flops 2157967360 | bytes 11542528 | tf_op jit(solution)/shard_map/dot_general | solution.py:41
  55.5 2.7 %multiply_reduce_fusion.2 = f32[2048]{0:T(1024)S(1)} fusion(f32[2048,512]{0,1:T(8,128)} %get-tuple-element.326, f32[2048]{0:T(1024)S(1)} %broadcast_multiply_fusion.2), kind=kLoop, calls=%fused_computation.58 | loop fusion | flops 3143680 | bytes 4210688 | tf_op jit(solution)/shard_map/reduce_sum | solution.py:29
  58.2 4.4 %multiply_convert_fusion.5 = bf16[128,512]{1,0:T(8,128)(2,1)S(1)} fusion(f32[128,512]{1,0:T(8,128)S(1)} %copy-done.9, bf16[3,2,512,512]{3,2,1,0:T(8,128)(2,1)} %param.38, bf16[2048,512]{0,1:T(8,128)(2,1)} %copy.16, f32[2048,512]{0,1:T(8,128)} %get-tuple-element.326, f32[512]{0:T(512)S(1)} %bitcast.242, f32[512]{0:T(512)S(1)} %bitcast.243, ...), kind=kOutput, calls=%fused_computation.145 | convolution fusion | flops 343605248 | bytes 7237632 | tf_op jit(solution)/shard_map/dot_general | solution.py:47
  69.3 8.3 %all-to-all-start = ((bf16[32,16,512]{2,1,0:T(8,128)(2,1)}), bf16[32,16,512]{2,1,0:T(8,128)(2,1)S(1)}, u32[]{:S(2)}, u32[]{:S(2)}) async-start(bf16[32,16,512]{2,1,0:T(8,128)(2,1)} %bitcast.20), calls=%async_computation | async-start | bytes 1048576 | tf_op jit(solution)/shard_map/all_to_all | solution.py:114
  79.1 4.7 %while.77 = (s32[]{:T(128)}, bf16[4,512,512]{2,1,0:T(8,128)(2,1)}, s32[4,512]{1,0:T(4,128)S(1)}, bf16[128,512]{1,0:T(8,128)(2,1)S(1)}, s32[]{:T(128)}) while((s32[]{:T(128)}, bf16[4,512,512]{2,1,0:T(8,128)(2,1)}, s32[4,512]{1,0:T(4,128)S(1)}, bf16[128,512]{1,0:T(8,128)(2,1)S(1)}, s32[]{:T(128)}) %tuple.128), condition=%wide.region_11.12_spmd.clone, body=%wide.region_10.11_spmd.clone.sunk | while | flops 67436544 | bytes 662081 | solution.py:64
  83.8 10.0 %all-to-all-done = bf16[32,16,512]{2,1,0:T(8,128)(2,1)S(1)} async-done(((bf16[32,16,512]{2,1,0:T(8,128)(2,1)}), bf16[32,16,512]{2,1,0:T(8,128)(2,1)S(1)}, u32[]{:S(2)}, u32[]{:S(2)}) %all-to-all-start) | async-done | bytes 524320 | tf_op jit(solution)/shard_map/all_to_all | solution.py:114
  96.2 5.8 %while.76 = (s32[]{:T(128)}, bf16[4,512,512]{2,1,0:T(8,128)(2,1)}, s32[4,512]{1,0:T(4,128)S(1)}, bf16[640,512]{1,0:T(8,128)(2,1)S(1)}, s32[]{:T(128)}) while((s32[]{:T(128)}, bf16[4,512,512]{2,1,0:T(8,128)(2,1)}, s32[4,512]{1,0:T(4,128)S(1)}, bf16[640,512]{1,0:T(8,128)(2,1)S(1)}, s32[]{:T(128)}) %tuple.140), condition=%wide.region_9.10_spmd.clone, body=%wide.region_8.9_spmd.clone.sunk | while | flops 336134144 | bytes 1186369 | solution.py:64
  101.9 7.9 %fusion.121 = (f32[2048]{0:T(1024)S(1)}, f32[2048,512]{0,1:T(8,128)}) fusion(bf16[3,512,512]{2,1,0:T(8,128)(2,1)} %param.37, bf16[2048,512]{1,0:T(8,128)(2,1)} %bitcast.215, bf16[2048,512]{1,0:T(8,128)(2,1)} %bitcast.216, bf16[2048,512]{1,0:T(8,128)(2,1)} %param.32, bf16[3,3,512,512]{3,2,1,0:T(8,128)(2,1)} %param.36), kind=kOutput, calls=%fused_computation.169 | convolution fusion | flops 2157967360 | bytes 11542528 | tf_op jit(solution)/shard_map/dot_general | solution.py:41
  109.9 2.8 %multiply_reduce_fusion.1 = f32[2048]{0:T(1024)S(1)} fusion(f32[2048,512]{0,1:T(8,128)} %get-tuple-element.330, f32[2048]{0:T(1024)S(1)} %broadcast_multiply_fusion.1), kind=kLoop, calls=%fused_computation.55 | loop fusion | flops 3143680 | bytes 4210688 | tf_op jit(solution)/shard_map/reduce_sum | solution.py:29
  113.3 2.4 %add_convert_fusion.1 = bf16[2048,512]{0,1:T(8,128)(2,1)} fusion(bf16[2048,512]{0,1:T(8,128)(2,1)S(1)} %copy.17, f32[2048,512]{0,1:T(8,128)S(1)} %copy-done, f32[512]{0:T(512)S(1)} %bitcast.238, f32[512]{0:T(512)S(1)} %bitcast.239, f32[2048]{0:T(1024)S(1)} %add_rsqrt_fusion.1, f32[2048]{0:T(1024)S(1)} %broadcast_multiply_fusion.1), kind=kLoop, calls=%fused_computation.54 | loop fusion | flops 7340032 | bytes 8409088 | tf_op jit(solution)/shard_map/convert_element_type | solution.py:42
  115.7 2.7 %multiply_convert_fusion.4 = bf16[128,512]{1,0:T(8,128)(2,1)S(1)} fusion(f32[128,512]{1,0:T(8,128)S(1)} %fusion.61, bf16[3,2,512,512]{3,2,1,0:T(8,128)(2,1)} %param.38, bf16[2048,512]{0,1:T(8,128)(2,1)} %add_convert_fusion.1, s32[2048]{0:T(1024)S(1)} %bitcast.236), kind=kOutput, calls=%fused_computation.141 | convolution fusion | flops 336265216 | bytes 3022848 | tf_op jit(solution)/shard_map/dot_general | solution.py:47
  122.7 2.0 %fusion.51 = f32[128,512]{1,0:T(8,128)} fusion(bf16[128,512]{1,0:T(8,128)(2,1)S(1)} %add_convert_fusion.16, bf16[3,2,512,512]{3,2,1,0:T(8,128)(2,1)} %param.38), kind=kOutput, calls=%fused_computation.92 | convolution fusion | flops 67108864 | bytes 917504 | tf_op jit(solution)/shard_map/dot_general | solution.py:46
  125.9 2.8 %all-to-all-start.1 = ((bf16[32,16,512]{2,1,0:T(8,128)(2,1)}), bf16[32,16,512]{2,1,0:T(8,128)(2,1)S(1)}, u32[]{:S(2)}, u32[]{:S(2)}) async-start(bf16[32,16,512]{2,1,0:T(8,128)(2,1)} %bitcast.35), calls=%async_computation.1 | async-start | bytes 1048576 | tf_op jit(solution)/shard_map/all_to_all | solution.py:114
  128.9 1.5 while.79
  130.4 14.4 %all-to-all-done.1 = bf16[32,16,512]{2,1,0:T(8,128)(2,1)S(1)} async-done(((bf16[32,16,512]{2,1,0:T(8,128)(2,1)}), bf16[32,16,512]{2,1,0:T(8,128)(2,1)S(1)}, u32[]{:S(2)}, u32[]{:S(2)}) %all-to-all-start.1) | async-done | bytes 524320 | tf_op jit(solution)/shard_map/all_to_all | solution.py:114
  145.9 2.6 %while.78 = (s32[]{:T(128)}, bf16[4,512,512]{2,1,0:T(8,128)(2,1)S(1)}, s32[4,512]{1,0:T(4,128)S(1)}, bf16[640,512]{1,0:T(8,128)(2,1)S(1)}, s32[]{:T(128)}) while((s32[]{:T(128)}, bf16[4,512,512]{2,1,0:T(8,128)(2,1)S(1)}, s32[4,512]{1,0:T(4,128)S(1)}, bf16[640,512]{1,0:T(8,128)(2,1)S(1)}, s32[]{:T(128)}) %tuple.141), condition=%wide.region_17.18_spmd.clone, body=%wide.region_16.17_spmd.clone.sunk | while | flops 336134144 | bytes 1185861 | solution.py:64
  148.6 7.6 %fusion.125 = (f32[2048]{0:T(1024)S(1)}, f32[2048,512]{0,1:T(8,128)}) fusion(bf16[3,512,512]{2,1,0:T(8,128)(2,1)} %param.37, bf16[2048,512]{1,0:T(8,128)(2,1)} %bitcast.217, bf16[2048,512]{1,0:T(8,128)(2,1)S(1)} %bitcast.212, bf16[2048,512]{0,1:T(8,128)(2,1)} %add_convert_fusion.1, bf16[3,3,512,512]{3,2,1,0:T(8,128)(2,1)} %param.36), kind=kOutput, calls=%fused_computation.171 | convolution fusion | flops 2157967360 | bytes 11542528 | tf_op jit(solution)/shard_map/dot_general | solution.py:41
  156.2 2.8 %multiply_reduce_fusion = f32[2048]{0:T(1024)S(1)} fusion(f32[2048,512]{0,1:T(8,128)} %get-tuple-element.334, f32[2048]{0:T(1024)S(1)} %broadcast_multiply_fusion), kind=kLoop, calls=%fused_computation.52 | loop fusion | flops 3143680 | bytes 4210688 | tf_op jit(solution)/shard_map/reduce_sum | solution.py:29
  159.1 3.8 %multiply_convert_fusion.3 = bf16[128,512]{1,0:T(8,128)(2,1)S(1)} fusion(f32[128,512]{1,0:T(8,128)S(1)} %copy-done.8, bf16[3,2,512,512]{3,2,1,0:T(8,128)(2,1)} %param.38, bf16[2048,512]{0,1:T(8,128)(2,1)S(1)} %copy-done.4, f32[2048,512]{0,1:T(8,128)} %get-tuple-element.334, f32[512]{0:T(512)S(1)} %bitcast.240, f32[512]{0:T(512)S(1)} %bitcast.241, ...), kind=kOutput, calls=%fused_computation.138 | convolution fusion | flops 343605248 | bytes 7237632 | tf_op jit(solution)/shard_map/dot_general | solution.py:47
  (140 shorter events, 48.1 us)
Async XLA Ops:
  0.8 17.4 %collective-permute-start = (bf16[4,4,512]{2,1,0:T(4,128)(2,1)S(1)}, bf16[4,4,512]{2,1,0:T(4,128)(2,1)S(1)}, u32[]{:S(2)}, u32[]{:S(2)}) collective-permute-start(bf16[4,4,512]{2,1,0:T(4,128)(2,1)S(1)} %get-tuple-element.311), channel_id=1, source_target_pairs={{0,1},{1,2},{2,3},{3,4},{4,5},{5,6},{6,7},{7,0},{8,9},{9,10},{10,1... | collective-permute-start | bytes 49160 | tf_op jit(solution)/shard_map/ppermute | solution.py:21
  3.8 14.4 %collective-permute-start.1 = (bf16[4,4,512]{2,1,0:T(4,128)(2,1)S(1)}, bf16[4,4,512]{2,1,0:T(4,128)(2,1)S(1)}, u32[]{:S(2)}, u32[]{:S(2)}) collective-permute-start(bf16[4,4,512]{2,1,0:T(4,128)(2,1)S(1)} %get-tuple-element.312), channel_id=1, source_target_pairs={{1,0},{2,1},{3,2},{4,3},{5,4},{6,5},{7,6},{0,7},{9,8},{10,9},{11,1... | collective-permute-start | bytes 49160 | tf_op jit(solution)/shard_map/ppermute | solution.py:22
  10.4 1.6 copy-start.10
  10.4 2.2 %copy-start.13 = (s32[1,2048]{1,0:T(1,128)S(1)}, s32[1,2048]{1,0:T(1,128)}, u32[]{:S(2)}) copy-start(s32[1,2048]{1,0:T(1,128)} %param.30) | copy-start | bytes 24580
  12.0 1.4 copy-start.2
  13.4 4.1 %copy-start.14 = (s32[1,2048]{1,0:T(1,128)S(1)}, s32[1,2048]{1,0:T(1,128)}, u32[]{:S(2)}) copy-start(s32[1,2048]{1,0:T(1,128)} %param.33) | copy-start | bytes 24580
  13.4 4.8 %copy-start.1 = (bf16[4,128,512]{2,1,0:T(8,128)(2,1)S(1)}, bf16[4,128,512]{2,1,0:T(8,128)(2,1)}, u32[]{:S(2)}) copy-start(bf16[4,128,512]{2,1,0:T(8,128)(2,1)} %param.27) | copy-start | bytes 1572868
  13.4 8.6 %copy-start.16 = (s32[1,2048]{1,0:T(1,128)S(1)}, s32[1,2048]{1,0:T(1,128)}, u32[]{:S(2)}) copy-start(s32[1,2048]{1,0:T(1,128)} %param.34) | copy-start | bytes 24580
  19.2 8.5 %collective-permute-start.2 = (bf16[4,136,512]{2,1,0:T(8,128)(2,1)}, bf16[4,136,512]{2,1,0:T(8,128)(2,1)S(1)}, u32[]{:S(2)}, u32[]{:S(2)}) collective-permute-start(bf16[4,136,512]{2,1,0:T(8,128)(2,1)} %pad_maximum_fusion.3), channel_id=1, source_target_pairs={{0,8},{8,16},{16,24},{1,9},{9,17},{17,25},{2,10},{10,18},{18,26},{... | collective-permute-start | bytes 1671176 | tf_op jit(solution)/shard_map/ppermute | solution.py:21
  20.7 7.0 %collective-permute-start.3 = (bf16[4,136,512]{2,1,0:T(8,128)(2,1)}, bf16[4,136,512]{2,1,0:T(8,128)(2,1)}, u32[]{:S(2)}, u32[]{:S(2)}) collective-permute-start(bf16[4,136,512]{2,1,0:T(8,128)(2,1)} %pad_maximum_fusion.3), channel_id=1, source_target_pairs={{8,0},{16,8},{24,16},{9,1},{17,9},{25,17},{10,2},{18,10},{26,18},{... | collective-permute-start | bytes 1671176 | tf_op jit(solution)/shard_map/ppermute | solution.py:22
  22.0 3.0 %copy-start.11 = (f32[3,2,512]{2,1,0:T(2,128)S(1)}, f32[3,2,512]{2,1,0:T(2,128)}, u32[]{:S(2)}) copy-start(f32[3,2,512]{2,1,0:T(2,128)} %param.40) | copy-start | bytes 36868
  22.0 3.6 %copy-start.7 = (bf16[128,512]{1,0:T(8,128)(2,1)S(1)}, bf16[128,512]{1,0:T(8,128)(2,1)}, u32[]{:S(2)}) copy-start(bf16[128,512]{1,0:T(8,128)(2,1)} %param.28) | copy-start | bytes 393220
  55.5 2.7 %copy-start.9 = (f32[128,512]{1,0:T(8,128)S(1)}, f32[128,512]{1,0:T(8,128)}, u32[]{:S(2)}) copy-start(f32[128,512]{1,0:T(8,128)} %fusion.71) | copy-start | bytes 786436
  55.5 2.7 %copy-start.15 = (s32[1,2048]{1,0:T(1,128)S(1)}, s32[1,2048]{1,0:T(1,128)}, u32[]{:S(2)}) copy-start(s32[1,2048]{1,0:T(1,128)} %param.31) | copy-start | bytes 24580
  62.6 5.6 %copy-start.12 = (s32[1,512]{1,0:T(1,128)S(1)}, s32[1,512]{1,0:T(1,128)}, u32[]{:S(2)}) copy-start(s32[1,512]{1,0:T(1,128)} %param.35) | copy-start | bytes 6148
  69.3 24.5 %all-to-all-start = ((bf16[32,16,512]{2,1,0:T(8,128)(2,1)}), bf16[32,16,512]{2,1,0:T(8,128)(2,1)S(1)}, u32[]{:S(2)}, u32[]{:S(2)}) async-start(bf16[32,16,512]{2,1,0:T(8,128)(2,1)} %bitcast.20), calls=%async_computation | async-start | bytes 1048576 | tf_op jit(solution)/shard_map/all_to_all | solution.py:114
  94.7 1.5 copy-start.5
  109.9 3.4 %copy-start = (f32[2048,512]{0,1:T(8,128)S(1)}, f32[2048,512]{0,1:T(8,128)}, u32[]{:S(2)}) copy-start(f32[2048,512]{0,1:T(8,128)} %get-tuple-element.330) | copy-start | bytes 12582916
  121.4 4.5 %copy-start.6 = (bf16[128,512]{1,0:T(8,128)(2,1)}, bf16[128,512]{1,0:T(8,128)(2,1)S(1)}, u32[]{:S(2)}) copy-start(bf16[128,512]{1,0:T(8,128)(2,1)S(1)} %convolution_convert_fusion.7) | copy-start | bytes 393220
  125.9 19.0 %all-to-all-start.1 = ((bf16[32,16,512]{2,1,0:T(8,128)(2,1)}), bf16[32,16,512]{2,1,0:T(8,128)(2,1)S(1)}, u32[]{:S(2)}, u32[]{:S(2)}) async-start(bf16[32,16,512]{2,1,0:T(8,128)(2,1)} %bitcast.35), calls=%async_computation.1 | async-start | bytes 1048576 | tf_op jit(solution)/shard_map/all_to_all | solution.py:114
  130.4 14.4 %copy-start.3 = (bf16[4,512,512]{2,1,0:T(8,128)(2,1)}, bf16[4,512,512]{2,1,0:T(8,128)(2,1)S(1)}, u32[]{:S(2)}) copy-start(bf16[4,512,512]{2,1,0:T(8,128)(2,1)S(1)} %get-tuple-element.202) | copy-start | bytes 6291460
  156.2 2.9 %copy-start.4 = (bf16[2048,512]{0,1:T(8,128)(2,1)S(1)}, bf16[2048,512]{0,1:T(8,128)(2,1)}, u32[]{:S(2)}) copy-start(bf16[2048,512]{0,1:T(8,128)(2,1)} %add_convert_fusion.1) | copy-start | bytes 6291460
  156.2 2.9 %copy-start.8 = (f32[128,512]{1,0:T(8,128)S(1)}, f32[128,512]{1,0:T(8,128)}, u32[]{:S(2)}) copy-start(f32[128,512]{1,0:T(8,128)} %fusion.51) | copy-start | bytes 786436
  156.2 2.9 %copy-start.17 = (s32[1,2048]{1,0:T(1,128)S(1)}, s32[1,2048]{1,0:T(1,128)}, u32[]{:S(2)}) copy-start(s32[1,2048]{1,0:T(1,128)} %param.34) | copy-start | bytes 24580
  156.2 2.9 %copy-start.18 = (f32[1,1,512]{2,1,0:T(1,128)S(1)}, f32[1,1,512]{2,1,0:T(1,128)}, u32[]{:S(2)}) copy-start(f32[1,1,512]{2,1,0:T(1,128)} %get-tuple-element.324) | copy-start | bytes 6148
  156.2 2.9 %copy-start.19 = (f32[1,1,512]{2,1,0:T(1,128)S(1)}, f32[1,1,512]{2,1,0:T(1,128)}, u32[]{:S(2)}) copy-start(f32[1,1,512]{2,1,0:T(1,128)} %get-tuple-element.318) | copy-start | bytes 6148
where the time goes:
time: 166 us; the launch traced here: 165 us
  matrix products  85 us (51%)
  waiting for transfers between devices  24.4 us (15%)
  starting transfers between devices  20 us (12%)
  other arithmetic  19.2 us (12%)
  local copies, waits for them, and re-layouts  15.6 us (9%)
    dot_general x26, matrix products, one_block(): jnp.dot(selector, table, preferred_element_type=jnp.float32)  31.6 us
    all_to_all x2, waiting for transfers between devices, local(): lax.all_to_all(out_rows, ('lat', 'lon'), split_axis=0, concat_axis=0, til...  24.4 us
    dot_general x3, matrix products, edge_update(): output = jnp.dot(hidden, weights_out, preferred_element_type=jnp.float32)  23.5 us
    all_to_all x2, starting transfers between devices, local(): lax.all_to_all(out_rows, ('lat', 'lon'), split_axis=0, concat_axis=0, til...  11.1 us
    dot_general x3, matrix products, node_update(): jnp.dot(summed.astype(jnp.bfloat16), weights_in[1], preferred_element_typ...  10.8 us
    dot_general x6, matrix products, project(): jnp.dot(values, weights, preferred_element_type=jnp.float32)  9.76 us
    reduce_sum x6, other arithmetic, normalize(): spread = jnp.mean(jnp.square(values - centre), axis=-1, keepdims=True)  8.81 us
    unnamed x43, local copies, waits for them, and re-layouts  8.36 us
  transfers between devices with their start and end apart: 6, of which 2 were waited for; matrix products, arithmetic and copies ran while one was open for 15% of the time, Pallas kernels for 0%

commit v1 on v0

v1 whole, which is shorter than its diff:
```python
import functools

import jax
import jax.numpy as jnp
from jax import lax
from jax.experimental import pallas as pl
from jax.experimental.pallas import tpu as pltpu
from jax.sharding import PartitionSpec as P

HALO = 4
NORM_EPS = 1e-05
LANES = 128
ROWS = 256
GROUP = 2
MESH_IDS = pl.DeviceIdType.MESH
BF16 = jnp.bfloat16
F32 = jnp.float32


def dot(a, b):
    return jnp.dot(a, b, preferred_element_type=F32)


def silu(v):
    half = 0.5 * v
    return half + half * jnp.tanh(half)


def layer_norm(values, gain, bias):
    scale = 1.0 / values.shape[-1]
    centre = jnp.sum(values, axis=-1, keepdims=True) * scale
    away = values - centre
    spread = jnp.sum(away * away, axis=-1, keepdims=True) * scale
    return away * lax.rsqrt(spread + NORM_EPS) * gain + bias


def onehot(idx, base, width):
    lane = lax.broadcasted_iota(jnp.int32, idx.shape, 1)
    parts = [
        jnp.where(idx == lane + (base + j), 1.0, 0.0).astype(BF16)
        for j in range(0, width, LANES)
    ]
    return parts[0] if len(parts) == 1 else jnp.concatenate(parts, axis=1)


def kernel(
    n_lat, n_lon, tile_rows, tile_cols, blocks,
    grid_hbm, mesh_ref, g2m_hbm, g2m_s_ref, g2m_r_ref, mm_hbm, mm_s_ref, mm_r_ref, send_ref,
    ein_hbm, eout_hbm, nin_hbm, nout_hbm, gain_ref, bias_ref,
    out_ref,
    grid_v, edge_v, mme_v, pre, tab, stk, wproj, eout, nin, nout,
    packs, picks, sel_send, idx_a, idx_b, idx_c, idx_d, nodes,
    w_sem, halo_send, halo_recv, a2a_send, a2a_recv,
):
    lat, lon = lax.axis_index("lat"), lax.axis_index("lon")
    n_dev = n_lat * n_lon
    me = lat * n_lon + lon
    width = mesh_ref.shape[1]
    node_count = mesh_ref.shape[0]
    cells = tile_rows * tile_cols
    cap = send_ref.shape[1] // n_dev
    barrier = pltpu.get_barrier_semaphore()

    def place(d):
        return (d // n_lon, d % n_lon)

    def greet(off, carry):
        d = (me + off) % n_dev
        pl.semaphore_signal(barrier, inc=1, device_id=place(d), device_id_type=MESH_IDS)
        return carry

    lax.fori_loop(1, n_dev, greet, 0)

    def load(src, dst, at):
        copy = pltpu.make_async_copy(src, dst, w_sem.at[at])
        copy.start()
        return copy

    own_at, north_at, south_at = width, width + cells, width + 2 * cells
    side_at = width + 3 * cells
    recv_at = side_at + LANES

    c_grid = load(grid_hbm, grid_v, 0)
    c_proj0 = load(ein_hbm.at[0, 1], wproj.at[0, 0], 1)
    c_w0 = load(ein_hbm.at[0, 0], tab.at[pl.ds(0, width)], 2)
    c_g2m = load(g2m_hbm, edge_v, 3)
    c_recv0 = load(ein_hbm.at[0, 2], wproj.at[0, 1], 4)

    tall = tile_rows + 2 * HALO
    wide = tile_cols + 2 * HALO
    zero_rows = functools.partial(jnp.zeros, dtype=BF16)
    side_rows = 2 * tall * HALO
    tab[side_at + side_rows:recv_at, :] = zero_rows((LANES - side_rows, width))
    block = tile_rows * HALO

    @pl.when(lat == 0)
    def _():
        tab[north_at:north_at + cells, :] = zero_rows((cells, width))
        tab[side_at:side_at + block, :] = zero_rows((block, width))
        tab[side_at + 3 * block:side_at + 4 * block, :] = zero_rows((block, width))

    @pl.when(lat == n_lat - 1)
    def _():
        tab[south_at:south_at + cells, :] = zero_rows((cells, width))
        tab[side_at + 2 * block:side_at + 3 * block, :] = zero_rows((block, width))
        tab[side_at + 5 * block:side_at + 6 * block, :] = zero_rows((block, width))

    c_grid.wait()
    c_proj0.wait()
    firsts, lasts = [], []
    for r in range(tile_rows):
        term = dot(grid_v[r], wproj[0, 0])
        tab[own_at + r * tile_cols:own_at + (r + 1) * tile_cols, :] = term.astype(BF16)
        firsts.append(term[:HALO])
        lasts.append(term[tile_cols - HALO:])
    packs[0:block, :] = jnp.concatenate(firsts, axis=0).astype(BF16)
    packs[block:2 * block, :] = jnp.concatenate(lasts, axis=0).astype(BF16)

    pl.semaphore_wait(barrier, n_dev - 1)

    own = tab.at[pl.ds(own_at, cells)]
    east, west = (lon + 1) % n_lon, (lon + n_lon - 1) % n_lon

    def halo(at, src, dst_row, count, to):
        return pltpu.make_async_remote_copy(
            src_ref=src, dst_ref=tab.at[pl.ds(dst_row, count)],
            send_sem=halo_send.at[at], recv_sem=halo_recv.at[at],
            device_id=to, device_id_type=MESH_IDS,
        )

    first_cols, last_cols = packs.at[pl.ds(0, block)], packs.at[pl.ds(block, block)]
    to_north = [
        halo(0, own, south_at, cells, (lat - 1, lon)),
        halo(1, last_cols, side_at + 2 * block, block, (lat - 1, east)),
        halo(2, first_cols, side_at + 5 * block, block, (lat - 1, west)),
    ]
    to_south = [
        halo(3, own, north_at, cells, (lat + 1, lon)),
        halo(4, last_cols, side_at, block, (lat + 1, east)),
        halo(5, first_cols, side_at + 3 * block, block, (lat + 1, west)),
    ]
    to_level = [
        halo(6, last_cols, side_at + block, block, (lat, east)),
        halo(7, first_cols, side_at + 4 * block, block, (lat, west)),
    ]

    @pl.when(lat > 0)
    def _():
        for c in to_north:
            c.start()

    @pl.when(lat < n_lat - 1)
    def _():
        for c in to_south:
            c.start()

    for c in to_level:
        c.start()

    c_eout, c_nin, c_nout, c_w, c_ps, c_pr = [], [], [], [None], [None], [None]
    at = 5
    for k in range(blocks):
        if k == 1:
            c_mm = load(mm_hbm, mme_v, at)
            at += 1
        if k > 0:
            c_ps.append(load(ein_hbm.at[k, 1], wproj.at[k, 0], at))
            c_pr.append(load(ein_hbm.at[k, 2], wproj.at[k, 1], at + 1))
            c_w.append(load(ein_hbm.at[k, 0], stk.at[k - 1, pl.ds(0, width)], at + 2))
            at += 3
        c_eout.append(load(eout_hbm.at[k], eout.at[k], at))
        c_nin.append(load(nin_hbm.at[k], nin.at[k], at + 1))
        c_nout.append(load(nout_hbm.at[k], nout.at[k], at + 2))
        at += 3

    senders = g2m_s_ref[...]
    row = jnp.zeros_like(senders)
    for r in range(1, tall):
        row = row + jnp.where(senders >= r * wide, 1, 0)
    col = senders - row * wide
    west_spot = 3 * cells + row * HALO + col
    east_spot = 3 * cells + (tall + row) * HALO + (col - (wide - HALO))
    spot = jnp.where(
        col < HALO, west_spot,
        jnp.where(col >= wide - HALO, east_spot, row * tile_cols + col - HALO),
    )

    def spread_rows(values, dst):
        for j in range(0, values.shape[1], LANES):
            piece = jnp.broadcast_to(values[:, j:j + LANES], (LANES, LANES))
            dst[j:j + LANES, :] = piece.T

    spread_rows(spot, idx_a)
    spread_rows(g2m_r_ref[...], idx_b)
    spread_rows(mm_s_ref[...], idx_c)
    spread_rows(jnp.minimum(mm_r_ref[...], node_count - 1), idx_d)
    sends = send_ref[...]
    for j in range(0, sends.shape[1], LANES):
        piece = jnp.broadcast_to(sends[:, j:j + LANES], (LANES, LANES)).T
        sel_send[j:j + LANES, :] = onehot(piece, 0, node_count)

    def over_rows(count, body):
        def step(i, carry):
            for g in range(GROUP):
                body(pl.ds(pl.multiple_of((i * GROUP + g) * ROWS, ROWS), ROWS))
            return carry

        lax.fori_loop(0, count // (ROWS * GROUP), step, 0)

    def finish_edges(rows, acc, edges, k):
        hidden = silu(acc).astype(BF16)
        normed = layer_norm(dot(hidden, eout[k]), gain_ref[k, 0:1, :], bias_ref[k, 0:1, :])
        edges[rows, :] = (edges[rows, :].astype(F32) + normed).astype(BF16)

    def gather_sum(recv_ref, edges):
        node = lax.broadcasted_iota(jnp.int32, (node_count, recv_ref.shape[1]), 0)
        incidence = jnp.where(node == recv_ref[...], 1.0, 0.0).astype(BF16)
        return dot(incidence, edges[...])

    def node_step(current, summed, k):
        c_nin[k].wait()
        c_nout[k].wait()
        joined = jnp.concatenate([current, summed.astype(BF16)], axis=1)
        hidden = silu(dot(joined, nin[k])).astype(BF16)
        normed = layer_norm(dot(hidden, nout[k]), gain_ref[k, 1:2, :], bias_ref[k, 1:2, :])
        return (current.astype(F32) + normed).astype(BF16)

    c_w0.wait()
    c_g2m.wait()

    def enc_first(rows):
        joined = jnp.concatenate([edge_v[rows, :], onehot(idx_a[rows, :], cells, cells)], axis=1)
        pre[rows, :] = dot(joined, tab[0:width + cells, :])

    over_rows(edge_v.shape[0], enc_first)
    c_recv0.wait()
    tab[recv_at:recv_at + node_count, :] = dot(mesh_ref[...], wproj[0, 1]).astype(BF16)
    c_eout[0].wait()

    for c in to_level:
        c.wait()

    @pl.when(lat > 0)
    def _():
        for c in to_north:
            c.wait_send()
        for c in to_south:
            c.wait_recv()

    @pl.when(lat < n_lat - 1)
    def _():
        for c in to_south:
            c.wait_send()
        for c in to_north:
            c.wait_recv()

    def enc_second(rows):
        spots = idx_a[rows, :]
        joined = jnp.concatenate(
            [
                onehot(spots, 0, cells),
                onehot(spots, 2 * cells, cells + LANES),
                onehot(idx_b[rows, :], 0, node_count),
            ],
            axis=1,
        )
        acc = pre[rows, :] + dot(joined, tab[north_at:recv_at + node_count, :])
        finish_edges(rows, acc, edge_v, 0)

    over_rows(edge_v.shape[0], enc_second)
    nodes[...] = node_step(mesh_ref[...], gather_sum(g2m_r_ref, edge_v), 0)

    r_at, s_at, arr_at = width, width + node_count, width + 2 * node_count
    for k in range(1, blocks):
        table, pick = stk.at[k - 1], picks.at[k - 1]
        current = nodes[...]
        c_ps[k].wait()
        outgoing = dot(current, wproj[k, 0]).astype(BF16)
        pick[...] = dot(sel_send[...], outgoing).astype(BF16)

        def exchange(d, src_at, sem_at, to):
            return pltpu.make_async_remote_copy(
                src_ref=pick.at[pl.ds(pl.multiple_of(d * cap, cap), cap)],
                dst_ref=table.at[pl.ds(pl.multiple_of(arr_at + src_at * cap, cap), cap)],
                send_sem=a2a_send.at[k - 1, d], recv_sem=a2a_recv.at[k - 1, sem_at],
                device_id=place(to), device_id_type=MESH_IDS,
            )

        def send(off, carry):
            d = (me + off) % n_dev
            exchange(d, me, me, d).start()
            return carry

        lax.fori_loop(1, n_dev, send, 0)
        table[pl.ds(pl.multiple_of(arr_at + me * cap, cap), cap), :] = pick[
            pl.ds(pl.multiple_of(me * cap, cap), cap), :
        ]
        table[s_at:s_at + node_count, :] = outgoing
        c_pr[k].wait()
        table[r_at:r_at + node_count, :] = dot(current, wproj[k, 1]).astype(BF16)
        c_w[k].wait()
        if k == 1:
            c_mm.wait()

        def mm_first(rows):
            joined = jnp.concatenate(
                [
                    mme_v[rows, :],
                    onehot(idx_d[rows, :], 0, node_count),
                    onehot(idx_c[rows, :], 0, node_count),
                ],
                axis=1,
            )
            pre[rows, :] = dot(joined, table[0:arr_at, :])

        over_rows(mme_v.shape[0], mm_first)
        c_eout[k].wait()

        def arrive(off, carry):
            d = (me + off) % n_dev
            exchange(d, d, d, d).wait()
            return carry

        lax.fori_loop(1, n_dev, arrive, 0)

        def mm_second(rows):
            picked = onehot(idx_c[rows, :], node_count, n_dev * cap)
            acc = pre[rows, :] + dot(picked, table[arr_at:arr_at + n_dev * cap, :])
            finish_edges(rows, acc, mme_v, k)

        over_rows(mme_v.shape[0], mm_second)
        updated = node_step(current, gather_sum(mm_r_ref, mme_v), k)
        if k < blocks - 1:
            nodes[...] = updated
        else:
            out_ref[...] = updated


def local(
    n_lat, n_lon,
    grid_latent, mesh_latent, g2m_edges, g2m_senders, g2m_receivers, mm_edges, mm_senders,
    mm_receivers, send_rows, edge_in, edge_out, node_in, node_out, norm_gain, norm_bias,
):
    tile_rows, tile_cols, width = grid_latent.shape
    blocks = edge_in.shape[0]
    node_count = mesh_latent.shape[0]
    n_dev = n_lat * n_lon
    edges, mm = g2m_edges.shape[0], mm_edges.shape[0]
    sends = send_rows.shape[1]
    assert tile_rows == HALO and node_count == LANES and tile_cols % LANES == 0
    node_in = node_in.reshape(blocks, 2 * width, width)
    hbm, vmem = pl.BlockSpec(memory_space=pl.ANY), pl.BlockSpec(memory_space=pltpu.VMEM)
    table_rows = width + 3 * tile_rows * tile_cols + LANES + node_count
    dma = pltpu.SemaphoreType.DMA
    return pl.pallas_call(
        functools.partial(kernel, n_lat, n_lon, tile_rows, tile_cols, blocks),
        out_shape=jax.ShapeDtypeStruct((node_count, width), BF16),
        in_specs=[hbm, vmem, hbm, vmem, vmem, hbm, vmem, vmem, vmem, hbm, hbm, hbm, hbm, vmem, vmem],
        out_specs=vmem,
        scratch_shapes=[
            pltpu.VMEM((tile_rows, tile_cols, width), BF16),
            pltpu.VMEM((edges, width), BF16),
            pltpu.VMEM((mm, width), BF16),
            pltpu.VMEM((max(edges, mm), width), F32),
            pltpu.VMEM((table_rows, width), BF16),
            pltpu.VMEM((blocks - 1, width + 2 * node_count + sends, width), BF16),
            pltpu.VMEM((blocks, 2, width, width), BF16),
            pltpu.VMEM((blocks, width, width), BF16),
            pltpu.VMEM((blocks, 2 * width, width), BF16),
            pltpu.VMEM((blocks, width, width), BF16),
            pltpu.VMEM((2 * tile_rows * HALO, width), BF16),
            pltpu.VMEM((blocks - 1, sends, width), BF16),
            pltpu.VMEM((sends, node_count), BF16),
            pltpu.VMEM((edges, LANES), jnp.int32),
            pltpu.VMEM((edges, LANES), jnp.int32),
            pltpu.VMEM((mm, LANES), jnp.int32),
            pltpu.VMEM((mm, LANES), jnp.int32),
            pltpu.VMEM((node_count, width), BF16),
            dma((6 + 6 * blocks,)),
            dma((8,)),
            dma((8,)),
            dma((blocks - 1, n_dev)),
            dma((blocks - 1, n_dev)),
        ],
        compiler_params=pltpu.CompilerParams(
            collective_id=0, has_side_effects=True, vmem_limit_bytes=56 * 1024 * 1024
        ),
        name="encode_process",
    )(
        grid_latent, mesh_latent, g2m_edges, g2m_senders, g2m_receivers, mm_edges, mm_senders,
        mm_receivers, send_rows, edge_in, edge_out, node_in, node_out, norm_gain, norm_bias,
    )


def solution(mesh):
    tiles = P(("lat", "lon"), None)
    in_specs = (P("lat", "lon", None),) + (tiles,) * 8 + (P(),) * 6
    body = functools.partial(local, mesh.shape["lat"], mesh.shape["lon"])
    return jax.shard_map(body, mesh=mesh, in_specs=in_specs, out_specs=tiles, check_vma=False)
```

time: 166 us -> 64.2 us (0.39)
  matrix products: 85 us -> 0 us
  Pallas kernels: 0 us -> 62.4 us
  waiting for transfers between devices: 24.4 us -> 0 us
  starting transfers between devices: 20 us -> 0 us
  other arithmetic: 19.2 us -> 0 us
  local copies, waits for them, and re-layouts: 15.6 us -> 1.57 us
    dot_general x44 -> x0, matrix products: 85 us -> none  [the longest x26 31.6 us: one_block(): jnp.dot(selector, table, preferred_element_type=jnp.float32)]
    pallas_call x0 -> x1, Pallas kernels: none -> 62.4 us  [local(): pl.pallas_call(functools.partial(kernel, n_lat, n_lon, tile_rows, tile_co...]
    all_to_all x2 -> x0, waiting for transfers between devices: 24.4 us -> none  [local(): lax.all_to_all(out_rows, ('lat', 'lon'), split_axis=0, concat_axis=0, til...]
    all_to_all x2 -> x0, starting transfers between devices: 11.1 us -> none  [local(): lax.all_to_all(out_rows, ('lat', 'lon'), split_axis=0, concat_axis=0, til...]
    ppermute x4 -> x0, starting transfers between devices: 8.9 us -> none  [the longest x2 4.5 us: padded_2(): before = lax.ppermute(last, axis, up)]
    reduce_sum x6 -> x0, other arithmetic: 8.81 us -> none  [normalize(): spread = jnp.mean(jnp.square(values - centre), axis=-1, keepdims=True)]
    unnamed x43 -> x1, local copies, waits for them, and re-layouts: 8.36 us -> 1.57 us
    another operation x9 -> x0, local copies, waits for them, and re-layouts: 5.06 us -> none
  transfers between devices with their start and end apart: 6 -> 0, of which waited for: 2 -> 0; matrix products, arithmetic and copies ran while one was open for 15% -> 0% of each run, Pallas kernels for 0% -> 0%
where the time goes in v1:
time: 64.2 us; the launch traced here: 64 us
  Pallas kernels  62.4 us (97%)
  local copies, waits for them, and re-layouts  1.57 us (2%)
    pallas_call x1, Pallas kernels, local(): pl.pallas_call(functools.partial(kernel, n_lat, n_lon, tile_rows, tile_co...  62.4 us
    unnamed x1, local copies, waits for them, and re-layouts  1.57 us

profile of v1, /device:TPU:0, one launch (start us, length us, event | category | flops | bytes accessed | tf_op | source)
XLA Modules:
  0.0 64.0 jit_solution(17044055327492906940)
XLA Ops:
  0.0 62.4 %encode_process.1 = bf16[128,512]{1,0:T(8,128)(2,1)} custom-call(bf16[4,128,512]{2,1,0:T(8,128)(2,1)} %grid_hbm.1, bf16[128,512]{1,0:T(8,128)(2,1)} %mesh_ref.1, bf16[2048,512]{1,0:T(8,128)(2,1)} %g2m_hbm.1, s32[1,2048]{1,0:T(1,128)} %g2m_s_ref.1, s32[1,2048]{1,0:T(1,128)} %g2m_r_ref.1, bf16[2048,512]{1,0:T(8,128)(2,1)} %mm_hbm.1, s32[1,2048]{1,0:T(1,128)} %mm_s_ref.1, ...), custom_call_target="tpu_custom_call" | custom-call | tf_op jit(solution)/shard_map/encode_process/pallas_call | solution.py:355
  62.4 1.6 %copy.17 = bf16[128,512]{1,0:T(8,128)(2,1)} copy(bf16[128,512]{1,0:T(8,128)(2,1)} %encode_process.1) | data formatting | bytes 262144

commit v2 on v1

--- a/solution.py
+++ b/solution.py
@@ -1,4 +1,5 @@
 import functools
+import math
 
 import jax
 import jax.numpy as jnp
@@ -11,7 +12,7 @@
 NORM_EPS = 1e-05
 LANES = 128
 ROWS = 256
-GROUP = 2
+GROUP = 4
 MESH_IDS = pl.DeviceIdType.MESH
 BF16 = jnp.bfloat16
 F32 = jnp.float32
@@ -45,10 +46,11 @@
 
 def kernel(
     n_lat, n_lon, tile_rows, tile_cols, blocks,
-    grid_hbm, mesh_ref, g2m_hbm, g2m_s_ref, g2m_r_ref, mm_hbm, mm_s_ref, mm_r_ref, send_ref,
-    ein_hbm, eout_hbm, nin_hbm, nout_hbm, gain_ref, bias_ref,
+    grid_hbm, mesh_hbm, g2m_hbm, g2m_s_hbm, g2m_r_hbm, mm_hbm, mm_s_hbm, mm_r_hbm, send_hbm,
+    ein_hbm, eout_hbm, nin_hbm, nout_hbm, gain_hbm, bias_hbm,
     out_ref,
-    grid_v, edge_v, mme_v, pre, tab, stk, wproj, eout, nin, nout,
+    mesh_ref, g2m_s_ref, g2m_r_ref, mm_s_ref, mm_r_ref, send_ref, gain_ref, bias_ref,
+    sel_arr, inc_g, inc_m, sums, grid_v, edge_v, mme_v, pre, tab, stk, wproj, eout, nin, nout,
     packs, picks, sel_send, idx_a, idx_b, idx_c, idx_d, nodes,
     w_sem, halo_send, halo_recv, a2a_send, a2a_recv,
 ):
@@ -69,7 +71,6 @@
         pl.semaphore_signal(barrier, inc=1, device_id=place(d), device_id_type=MESH_IDS)
         return carry
 
-    lax.fori_loop(1, n_dev, greet, 0)
 
     def load(src, dst, at):
         copy = pltpu.make_async_copy(src, dst, w_sem.at[at])
@@ -85,6 +86,15 @@
     c_w0 = load(ein_hbm.at[0, 0], tab.at[pl.ds(0, width)], 2)
     c_g2m = load(g2m_hbm, edge_v, 3)
     c_recv0 = load(ein_hbm.at[0, 2], wproj.at[0, 1], 4)
+    small = [
+        load(src, dst, 5 + i)
+        for i, (src, dst) in enumerate((
+            (g2m_s_hbm, g2m_s_ref), (g2m_r_hbm, g2m_r_ref), (mm_s_hbm, mm_s_ref),
+            (mm_r_hbm, mm_r_ref), (send_hbm, send_ref), (mesh_hbm, mesh_ref),
+            (gain_hbm, gain_ref), (bias_hbm, bias_ref),
+        ))
+    ]
+    lax.fori_loop(1, n_dev, greet, 0)
 
     tall = tile_rows + 2 * HALO
     wide = tile_cols + 2 * HALO
@@ -144,21 +154,21 @@
         halo(7, first_cols, side_at + 4 * block, block, (lat, west)),
     ]
 
-    @pl.when(lat > 0)
-    def _():
-        for c in to_north:
-            c.start()
-
-    @pl.when(lat < n_lat - 1)
-    def _():
-        for c in to_south:
-            c.start()
-
     for c in to_level:
         c.start()
 
+    @pl.when(lat > 0)
+    def _():
+        for c in reversed(to_north):
+            c.start()
+
+    @pl.when(lat < n_lat - 1)
+    def _():
+        for c in reversed(to_south):
+            c.start()
+
     c_eout, c_nin, c_nout, c_w, c_ps, c_pr = [], [], [], [None], [None], [None]
-    at = 5
+    at = 5 + len(small)
     for k in range(blocks):
         if k == 1:
             c_mm = load(mm_hbm, mme_v, at)
@@ -173,6 +183,9 @@
         c_nout.append(load(nout_hbm.at[k], nout.at[k], at + 2))
         at += 3
 
+    for c in small:
+        c.wait()
+
     senders = g2m_s_ref[...]
     row = jnp.zeros_like(senders)
     for r in range(1, tall):
@@ -207,15 +220,37 @@
 
         lax.fori_loop(0, count // (ROWS * GROUP), step, 0)
 
-    def finish_edges(rows, acc, edges, k):
-        hidden = silu(acc).astype(BF16)
-        normed = layer_norm(dot(hidden, eout[k]), gain_ref[k, 0:1, :], bias_ref[k, 0:1, :])
-        edges[rows, :] = (edges[rows, :].astype(F32) + normed).astype(BF16)
-
-    def gather_sum(recv_ref, edges):
-        node = lax.broadcasted_iota(jnp.int32, (node_count, recv_ref.shape[1]), 0)
-        incidence = jnp.where(node == recv_ref[...], 1.0, 0.0).astype(BF16)
-        return dot(incidence, edges[...])
+    def mark_receivers(recv_ref, dst):
+        node = lax.broadcasted_iota(jnp.int32, dst.shape, 0)
+        dst[...] = jnp.where(node == recv_ref[...], 1.0, 0.0).astype(BF16)
+
+    def finish_edges(first, edges, incidence, k):
+        sums[...] = jnp.zeros_like(sums)
+        gain, bias = gain_ref[k, 0:1, :], bias_ref[k, 0:1, :]
+
+        def step(i, carry):
+            spans = [
+                pl.ds(pl.multiple_of((i * GROUP + g) * ROWS, ROWS), ROWS) for g in range(GROUP)
+            ]
+            total = sums[...]
+            done = []
+            ahead = first(spans[0])
+            for g, rows in enumerate(spans):
+                acc = ahead
+                if g + 1 < GROUP:
+                    ahead = first(spans[g + 1])
+                hidden = silu(acc).astype(BF16)
+                normed = layer_norm(dot(hidden, eout[k]), gain, bias)
+                new = (edges[rows, :].astype(F32) + normed).astype(BF16)
+                total = total + dot(incidence[:, rows], new)
+                done.append(new)
+            for rows, new in zip(spans, done):
+                edges[rows, :] = new
+            sums[...] = total
+            return carry
+
+        lax.fori_loop(0, edges.shape[0] // (ROWS * GROUP), step, 0)
+        return sums[...]
 
     def node_step(current, summed, k):
         c_nin[k].wait()
@@ -223,7 +258,7 @@
         joined = jnp.concatenate([current, summed.astype(BF16)], axis=1)
         hidden = silu(dot(joined, nin[k])).astype(BF16)
         normed = layer_norm(dot(hidden, nout[k]), gain_ref[k, 1:2, :], bias_ref[k, 1:2, :])
-        return (current.astype(F32) + normed).astype(BF16)
+        return current.astype(F32) + normed
 
     c_w0.wait()
     c_g2m.wait()
@@ -237,39 +272,73 @@
     tab[recv_at:recv_at + node_count, :] = dot(mesh_ref[...], wproj[0, 1]).astype(BF16)
     c_eout[0].wait()
 
+    mark_receivers(g2m_r_ref, inc_g)
+
+    even = lat % 2 == 0
+    up, down = lat > 0, lat < n_lat - 1
+    near = jnp.where(even, 2 * cells, 0)
+    far = 2 * cells - near
+
+    def tile_part(spot_base):
+        start = jnp.where(spot_base == 0, north_at, south_at)
+        return tab[pl.ds(pl.multiple_of(start, cells), cells), :]
+
     for c in to_level:
         c.wait()
 
-    @pl.when(lat > 0)
+    @pl.when(up)
+    def _():
+        for c in to_south[1:]:
+            c.wait_recv()
+
+    @pl.when(down)
+    def _():
+        for c in to_north[1:]:
+            c.wait_recv()
+
+    @pl.when(jnp.logical_and(even, down))
+    def _():
+        to_north[0].wait_recv()
+
+    @pl.when(jnp.logical_not(even))
+    def _():
+        to_south[0].wait_recv()
+
+    def enc_near(rows):
+        spots = idx_a[rows, :]
+        rest = jnp.concatenate(
+            [onehot(spots, 3 * cells, LANES), onehot(idx_b[rows, :], 0, node_count)], axis=1
+        )
+        acc = pre[rows, :] + dot(rest, tab[side_at:recv_at + node_count, :])
+        pre[rows, :] = acc + dot(onehot(spots, near, cells), tile_part(near))
+
+    over_rows(edge_v.shape[0], enc_near)
+
+    @pl.when(jnp.logical_and(even, up))
+    def _():
+        to_south[0].wait_recv()
+
+    @pl.when(jnp.logical_and(jnp.logical_not(even), down))
+    def _():
+        to_north[0].wait_recv()
+
+    def enc_far(rows):
+        return pre[rows, :] + dot(onehot(idx_a[rows, :], far, cells), tile_part(far))
+
+    summed = finish_edges(enc_far, edge_v, inc_g, 0)
+    nodes[...] = node_step(mesh_ref[...], summed, 0).astype(BF16)
+
+    @pl.when(up)
     def _():
         for c in to_north:
             c.wait_send()
-        for c in to_south:
-            c.wait_recv()
-
-    @pl.when(lat < n_lat - 1)
+
+    @pl.when(down)
     def _():
         for c in to_south:
             c.wait_send()
-        for c in to_north:
-            c.wait_recv()
-
-    def enc_second(rows):
-        spots = idx_a[rows, :]
-        joined = jnp.concatenate(
-            [
-                onehot(spots, 0, cells),
-                onehot(spots, 2 * cells, cells + LANES),
-                onehot(idx_b[rows, :], 0, node_count),
-            ],
-            axis=1,
-        )
-        acc = pre[rows, :] + dot(joined, tab[north_at:recv_at + node_count, :])
-        finish_edges(rows, acc, edge_v, 0)
-
-    over_rows(edge_v.shape[0], enc_second)
-    nodes[...] = node_step(mesh_ref[...], gather_sum(g2m_r_ref, edge_v), 0)
-
+
+    stride = next(i for i in range(n_dev // 3 + 1, 2 * n_dev) if math.gcd(i, n_dev) == 1)
     r_at, s_at, arr_at = width, width + node_count, width + 2 * node_count
     for k in range(1, blocks):
         table, pick = stk.at[k - 1], picks.at[k - 1]
@@ -287,7 +356,7 @@
             )
 
         def send(off, carry):
-            d = (me + off) % n_dev
+            d = (me + off * stride) % n_dev
             exchange(d, me, me, d).start()
             return carry
 
@@ -314,24 +383,29 @@
             pre[rows, :] = dot(joined, table[0:arr_at, :])
 
         over_rows(mme_v.shape[0], mm_first)
+        if k == 1:
+            mark_receivers(mm_r_ref, inc_m)
+
+            def mark_arrived(rows):
+                sel_arr[rows, :] = onehot(idx_c[rows, :], node_count, n_dev * cap)
+
+            over_rows(mme_v.shape[0], mark_arrived)
         c_eout[k].wait()
 
         def arrive(off, carry):
-            d = (me + off) % n_dev
+            d = (me + off * stride) % n_dev
             exchange(d, d, d, d).wait()
             return carry
 
         lax.fori_loop(1, n_dev, arrive, 0)
 
         def mm_second(rows):
-            picked = onehot(idx_c[rows, :], node_count, n_dev * cap)
-            acc = pre[rows, :] + dot(picked, table[arr_at:arr_at + n_dev * cap, :])
-            finish_edges(rows, acc, mme_v, k)
-
-        over_rows(mme_v.shape[0], mm_second)
-        updated = node_step(current, gather_sum(mm_r_ref, mme_v), k)
+            return pre[rows, :] + dot(sel_arr[rows, :], table[arr_at:arr_at + n_dev * cap, :])
+
+        summed = finish_edges(mm_second, mme_v, inc_m, k)
+        updated = node_step(current, summed, k)
         if k < blocks - 1:
-            nodes[...] = updated
+            nodes[...] = updated.astype(BF16)
         else:
             out_ref[...] = updated
 
@@ -352,12 +426,24 @@
     hbm, vmem = pl.BlockSpec(memory_space=pl.ANY), pl.BlockSpec(memory_space=pltpu.VMEM)
     table_rows = width + 3 * tile_rows * tile_cols + LANES + node_count
     dma = pltpu.SemaphoreType.DMA
-    return pl.pallas_call(
+    done = pl.pallas_call(
         functools.partial(kernel, n_lat, n_lon, tile_rows, tile_cols, blocks),
-        out_shape=jax.ShapeDtypeStruct((node_count, width), BF16),
-        in_specs=[hbm, vmem, hbm, vmem, vmem, hbm, vmem, vmem, vmem, hbm, hbm, hbm, hbm, vmem, vmem],
+        out_shape=jax.ShapeDtypeStruct((node_count, width), F32),
+        in_specs=[hbm] * 15,
         out_specs=vmem,
         scratch_shapes=[
+            pltpu.VMEM(mesh_latent.shape, BF16),
+            pltpu.VMEM((1, edges), jnp.int32),
+            pltpu.VMEM((1, edges), jnp.int32),
+            pltpu.VMEM((1, mm), jnp.int32),
+            pltpu.VMEM((1, mm), jnp.int32),
+            pltpu.VMEM((1, sends), jnp.int32),
+            pltpu.VMEM(norm_gain.shape, F32),
+            pltpu.VMEM(norm_bias.shape, F32),
+            pltpu.VMEM((mm, sends), BF16),
+            pltpu.VMEM((node_count, edges), BF16),
+            pltpu.VMEM((node_count, mm), BF16),
+            pltpu.VMEM((node_count, width), F32),
             pltpu.VMEM((tile_rows, tile_cols, width), BF16),
             pltpu.VMEM((edges, width), BF16),
             pltpu.VMEM((mm, width), BF16),
@@ -376,7 +462,7 @@
             pltpu.VMEM((mm, LANES), jnp.int32),
             pltpu.VMEM((mm, LANES), jnp.int32),
             pltpu.VMEM((node_count, width), BF16),
-            dma((6 + 6 * blocks,)),
+            dma((14 + 6 * blocks,)),
             dma((8,)),
             dma((8,)),
             dma((blocks - 1, n_dev)),
@@ -390,6 +476,7 @@
         grid_latent, mesh_latent, g2m_edges, g2m_senders, g2m_receivers, mm_edges, mm_senders,
         mm_receivers, send_rows, edge_in, edge_out, node_in, node_out, norm_gain, norm_bias,
     )
+    return done.astype(BF16)
 
 
 def solution(mesh):

time: 64.2 us -> 65.9 us (1.026)
  the two profiles are of different devices: /device:TPU:0 before, /device:TPU:1 now
where the time goes in v2:
time: 65.9 us; the launch traced here: 65.8 us
  Pallas kernels  64.1 us (97%)
  other arithmetic  1.62 us (2%)
    pallas_call x1, Pallas kernels, local(): pl.pallas_call(functools.partial(kernel, n_lat, n_lon, tile_rows, tile_co...  64.1 us
    convert_element_type x1, other arithmetic, local(): return done.astype(BF16)  1.62 us

profile of v2, /device:TPU:1, one launch (start us, length us, event | category | flops | bytes accessed | tf_op | source)
XLA Modules:
  0.0 65.8 jit_solution(5263450215183896)
XLA Ops:
  0.0 64.1 %encode_process.1 = f32[128,512]{1,0:T(8,128)} custom-call(bf16[4,128,512]{2,1,0:T(8,128)(2,1)} %grid_hbm.1, bf16[128,512]{1,0:T(8,128)(2,1)} %mesh_hbm.1, bf16[2048,512]{1,0:T(8,128)(2,1)} %g2m_hbm.1, s32[1,2048]{1,0:T(1,128)} %g2m_s_hbm.1, s32[1,2048]{1,0:T(1,128)} %g2m_r_hbm.1, bf16[2048,512]{1,0:T(8,128)(2,1)} %mm_hbm.1, s32[1,2048]{1,0:T(1,128)} %mm_s_hbm.1, ...), custom_call_target="tpu_custom_call" | custom-call | tf_op jit(solution)/shard_map/encode_process/pallas_call | solution.py:429
  64.1 1.6 %convert_element_type.3 = bf16[128,512]{1,0:T(8,128)(2,1)} convert(f32[128,512]{1,0:T(8,128)} %encode_process.1) | non-fusion elementwise | flops 65536 | bytes 393216 | tf_op jit(solution)/shard_map/convert_element_type | solution.py:479

commit v3 on v2

--- a/solution.py
+++ b/solution.py
@@ -1,5 +1,4 @@
 import functools
-import math
 
 import jax
 import jax.numpy as jnp
@@ -12,7 +11,7 @@
 NORM_EPS = 1e-05
 LANES = 128
 ROWS = 256
-GROUP = 4
+GROUP = 2
 MESH_IDS = pl.DeviceIdType.MESH
 BF16 = jnp.bfloat16
 F32 = jnp.float32
@@ -50,7 +49,7 @@
     ein_hbm, eout_hbm, nin_hbm, nout_hbm, gain_hbm, bias_hbm,
     out_ref,
     mesh_ref, g2m_s_ref, g2m_r_ref, mm_s_ref, mm_r_ref, send_ref, gain_ref, bias_ref,
-    sel_arr, inc_g, inc_m, sums, grid_v, edge_v, mme_v, pre, tab, stk, wproj, eout, nin, nout,
+    sel_arr, inc_g, inc_m, sums, node_pre, grid_v, edge_v, mme_v, pre, tab, stk, wproj, eout, nin, nout,
     packs, picks, sel_send, idx_a, idx_b, idx_c, idx_d, nodes,
     w_sem, halo_send, halo_recv, a2a_send, a2a_recv,
 ):
@@ -252,11 +251,14 @@
         lax.fori_loop(0, edges.shape[0] // (ROWS * GROUP), step, 0)
         return sums[...]
 
-    def node_step(current, summed, k):
+    def node_first(current, k):
         c_nin[k].wait()
         c_nout[k].wait()
-        joined = jnp.concatenate([current, summed.astype(BF16)], axis=1)
-        hidden = silu(dot(joined, nin[k])).astype(BF16)
+        node_pre[...] = dot(current, nin[k, 0:width, :])
+
+    def node_step(current, summed, k):
+        acc = node_pre[...] + dot(summed.astype(BF16), nin[k, width:2 * width, :])
+        hidden = silu(acc).astype(BF16)
         normed = layer_norm(dot(hidden, nout[k]), gain_ref[k, 1:2, :], bias_ref[k, 1:2, :])
         return current.astype(F32) + normed
 
@@ -273,6 +275,7 @@
     c_eout[0].wait()
 
     mark_receivers(g2m_r_ref, inc_g)
+    node_first(mesh_ref[...], 0)
 
     even = lat % 2 == 0
     up, down = lat > 0, lat < n_lat - 1
@@ -338,7 +341,7 @@
         for c in to_south:
             c.wait_send()
 
-    stride = next(i for i in range(n_dev // 3 + 1, 2 * n_dev) if math.gcd(i, n_dev) == 1)
+    pending = []
     r_at, s_at, arr_at = width, width + node_count, width + 2 * node_count
     for k in range(1, blocks):
         table, pick = stk.at[k - 1], picks.at[k - 1]
@@ -347,17 +350,17 @@
         outgoing = dot(current, wproj[k, 0]).astype(BF16)
         pick[...] = dot(sel_send[...], outgoing).astype(BF16)
 
-        def exchange(d, src_at, sem_at, to):
+        def exchange(d):
             return pltpu.make_async_remote_copy(
                 src_ref=pick.at[pl.ds(pl.multiple_of(d * cap, cap), cap)],
-                dst_ref=table.at[pl.ds(pl.multiple_of(arr_at + src_at * cap, cap), cap)],
-                send_sem=a2a_send.at[k - 1, d], recv_sem=a2a_recv.at[k - 1, sem_at],
-                device_id=place(to), device_id_type=MESH_IDS,
+                dst_ref=table.at[pl.ds(pl.multiple_of(arr_at + me * cap, cap), cap)],
+                send_sem=a2a_send.at[k - 1], recv_sem=a2a_recv.at[k - 1],
+                device_id=place(d), device_id_type=MESH_IDS,
             )
 
         def send(off, carry):
-            d = (me + off * stride) % n_dev
-            exchange(d, me, me, d).start()
+            d = (me + off) % n_dev
+            exchange(d).start()
             return carry
 
         lax.fori_loop(1, n_dev, send, 0)
@@ -391,13 +394,16 @@
 
             over_rows(mme_v.shape[0], mark_arrived)
         c_eout[k].wait()
-
-        def arrive(off, carry):
-            d = (me + off * stride) % n_dev
-            exchange(d, d, d, d).wait()
-            return carry
-
-        lax.fori_loop(1, n_dev, arrive, 0)
+        node_first(current, k)
+
+        whole = pltpu.make_async_remote_copy(
+            src_ref=pick.at[pl.ds(0, (n_dev - 1) * cap)],
+            dst_ref=table.at[pl.ds(arr_at, (n_dev - 1) * cap)],
+            send_sem=a2a_send.at[k - 1], recv_sem=a2a_recv.at[k - 1],
+            device_id=place((me + 1) % n_dev), device_id_type=MESH_IDS,
+        )
+        whole.wait_recv()
+        pending.append(whole)
 
         def mm_second(rows):
             return pre[rows, :] + dot(sel_arr[rows, :], table[arr_at:arr_at + n_dev * cap, :])
@@ -408,6 +414,8 @@
             nodes[...] = updated.astype(BF16)
         else:
             out_ref[...] = updated
+    for whole in pending:
+        whole.wait_send()
 
 
 def local(
@@ -428,7 +436,7 @@
     dma = pltpu.SemaphoreType.DMA
     done = pl.pallas_call(
         functools.partial(kernel, n_lat, n_lon, tile_rows, tile_cols, blocks),
-        out_shape=jax.ShapeDtypeStruct((node_count, width), F32),
+        out_shape=pltpu.VMEM((node_count, width), F32),
         in_specs=[hbm] * 15,
         out_specs=vmem,
         scratch_shapes=[
@@ -443,6 +451,7 @@
             pltpu.VMEM((mm, sends), BF16),
             pltpu.VMEM((node_count, edges), BF16),
             pltpu.VMEM((node_count, mm), BF16),
+            pltpu.VMEM((node_count, width), F32),
             pltpu.VMEM((node_count, width), F32),
             pltpu.VMEM((tile_rows, tile_cols, width), BF16),
             pltpu.VMEM((edges, width), BF16),
@@ -465,8 +474,8 @@
             dma((14 + 6 * blocks,)),
             dma((8,)),
             dma((8,)),
-            dma((blocks - 1, n_dev)),
-            dma((blocks - 1, n_dev)),
+            dma((blocks - 1,)),
+            dma((blocks - 1,)),
         ],
         compiler_params=pltpu.CompilerParams(
             collective_id=0, has_side_effects=True, vmem_limit_bytes=56 * 1024 * 1024

time: 65.9 us -> 63.6 us (0.965)
  the two profiles are of different devices: /device:TPU:1 before, /device:TPU:0 now
where the time goes in v3:
time: 63.6 us; the launch traced here: 63.5 us
  Pallas kernels  62.8 us (99%)
  other arithmetic  0.67 us (1%)
    pallas_call x1, Pallas kernels, local(): pl.pallas_call(functools.partial(kernel, n_lat, n_lon, tile_rows, tile_co...  62.8 us

profile of v3, /device:TPU:0, one launch (start us, length us, event | category | flops | bytes accessed | tf_op | source)
XLA Modules:
  0.0 63.5 jit_solution(18067982344430047594)
XLA Ops:
  0.0 62.8 %encode_process.1 = f32[128,512]{1,0:T(8,128)S(1)} custom-call(bf16[4,128,512]{2,1,0:T(8,128)(2,1)} %grid_hbm.1, bf16[128,512]{1,0:T(8,128)(2,1)} %mesh_hbm.1, bf16[2048,512]{1,0:T(8,128)(2,1)} %g2m_hbm.1, s32[1,2048]{1,0:T(1,128)} %g2m_s_hbm.1, s32[1,2048]{1,0:T(1,128)} %g2m_r_hbm.1, bf16[2048,512]{1,0:T(8,128)(2,1)} %mm_hbm.1, s32[1,2048]{1,0:T(1,128)} %mm_s_hbm.1, ...), custom_call_target="tpu_custom_call" | custom-call | tf_op jit(solution)/shard_map/encode_process/pallas_call | solution.py:437
  62.8 0.7 %convert_element_type.3 = bf16[128,512]{1,0:T(8,128)(2,1)} convert(f32[128,512]{1,0:T(8,128)S(1)} %encode_process.1) | non-fusion elementwise | flops 65536 | bytes 393216 | tf_op jit(solution)/shard_map/convert_element_type | solution.py:488
